TPU v7x, 32 devices: a whole 2x2x4 slice. The times are simulated.
32 devices in a mesh: req: 8 (over y, x, core), exp: 4 (over z).
Axes of the slice: x: 2, y: 2, z: 4, core: 2. Of those that a mesh axis runs over, the one named last changes fastest.
Arguments:
- tokens: bfloat16 [4096, 2048], P(('req', 'exp')), may hold values from -6 to 6
- attn_gain: float32 [2048], replicated, may hold values from 0.1 to 1.9
- w_query: bfloat16 [2048, 2048], P(None, 'exp'), may hold values from -0.25 to 0.25
- w_key: bfloat16 [2048, 2048], P(None, 'exp'), may hold values from -0.125 to 0.125
- w_value: bfloat16 [2048, 2048], P(None, 'exp'), may hold values from -0.125 to 0.125
- w_out: bfloat16 [2048, 2048], P('exp'), may hold values from -0.375 to 0.375
- prefix_cache: bfloat16 [4, 1024, 2, 2048], P(None, 'req', None, 'exp'), may hold values from -205 to 205
- group_of: int32 [8], replicated, may hold values from 0 to 3
- lengths: int32 [8], replicated, may hold values from 1 to 512, 2560 in all
- moe_gain: float32 [2048], replicated, may hold values from 0.1 to 1.9
- w_gate: bfloat16 [32, 2048, 512], P(('req', 'exp')), may hold values from -0.125 to 0.125
- w_up: bfloat16 [32, 2048, 512], P(('req', 'exp')), may hold values from -0.125 to 0.125
- w_down: bfloat16 [32, 512, 2048], P(('req', 'exp')), may hold values from -0.25 to 0.25
- routes: int32 [4096, 8], P(('req', 'exp')), may hold values from 0 to 15, all different within a row; in each aligned block of 128 rows (0 to 127, 128 to 255, ...) at most 72 rows name the same one
- route_weights: float32 [4096, 8], P(('req', 'exp')), may hold values from 0.1 to 0.4
Outputs:
- layer_out: bfloat16 [4096, 2048], P(('req', 'exp'))
Inputs may be any that keep to these rules, and one draw needn't show every extreme that they name: `routes`: in the rows of one device no expert is named more than 72 times.
All inputs are finite; a program needn't handle non-finite values.
Results may differ from a plain program's by a relative error of at most 0.017.
Values may be sent and summed in bfloat16 or wider, within the bound.
A program may use at most 192 MiB of HBM per device.

v0:
```python
import math

import jax
import jax.numpy as jnp
from jax import lax
from jax.sharding import PartitionSpec as P

HD = 128
PREFIX = 1024


def norm_rows(values, gain):
    wide = values.astype(jnp.float32)
    return wide * lax.rsqrt(jnp.mean(wide * wide, axis=-1, keepdims=True) + 1e-05) * gain


def rotate(vectors, places):
    half = vectors.shape[-1] // 2
    freqs = 10000.0 ** (-(jnp.arange(half, dtype=jnp.float32) * 2.0) / vectors.shape[-1])
    angles = places[:, None] * freqs[None, :]
    cosine = jnp.cos(angles)[:, None, :]
    sine = jnp.sin(angles)[:, None, :]
    first = vectors[..., :half]
    second = vectors[..., half:]
    return jnp.concatenate(
        [first * cosine - second * sine, first * sine + second * cosine], axis=-1
    )


def on_device(
    tokens,
    attn_gain,
    w_query,
    w_key,
    w_value,
    w_out,
    prefix_cache,
    group_of,
    lengths,
    moe_gain,
    w_gate,
    w_up,
    w_down,
    routes,
    route_weights,
):
    rows_dev, width = tokens.shape
    exp_count = lax.axis_size("exp")
    req_count = lax.axis_size("req")
    exp_index = lax.axis_index("exp")
    req_index = lax.axis_index("req")
    local_width = w_query.shape[1]
    head_dim = HD
    local_heads = local_width // head_dim
    slot_count = rows_dev * exp_count
    normed = norm_rows(tokens, attn_gain).astype(jnp.bfloat16)
    joined = jnp.concatenate([w_query, w_key, w_value], axis=1)
    piece = lax.all_gather(normed, "exp", axis=0, tiled=True)
    count = piece.shape[0]
    mixed = jnp.dot(piece, joined, preferred_element_type=jnp.float32)
    places = (PREFIX + jnp.int32(0) + jnp.arange(count, dtype=jnp.int32)).astype(jnp.float32)
    query = rotate(mixed[:, :local_width].reshape(count, local_heads, head_dim), places).reshape(
        count, local_width
    )
    key = rotate(
        mixed[:, local_width : 2 * local_width].reshape(count, local_heads, head_dim), places
    ).reshape(count, local_width)
    projected = jnp.concatenate([query, key, mixed[:, 2 * local_width :]], axis=1).astype(
        jnp.bfloat16
    )
    outgoing = jnp.take(prefix_cache, group_of, axis=0)
    arrived = lax.all_to_all(outgoing, "req", split_axis=0, concat_axis=1, tiled=True)[0]
    prefix_len = arrived.shape[0]
    query = projected[:, :local_width].reshape(slot_count, local_heads, head_dim)
    keys = jnp.concatenate(
        [
            arrived[:, 0].reshape(prefix_len, local_heads, head_dim),
            projected[:, local_width : 2 * local_width].reshape(slot_count, local_heads, head_dim),
        ],
        axis=0,
    )
    values = jnp.concatenate(
        [
            arrived[:, 1].reshape(prefix_len, local_heads, head_dim),
            projected[:, 2 * local_width :].reshape(slot_count, local_heads, head_dim),
        ],
        axis=0,
    )
    scores = jnp.einsum(
        "qhd,khd->hqk", query, keys, preferred_element_type=jnp.float32
    ) / math.sqrt(head_dim)
    length = lengths[req_index]
    live = jnp.concatenate(
        [jnp.ones((prefix_len,), bool), jnp.arange(slot_count, dtype=jnp.int32) < length]
    )
    scores = jnp.where(live[None, None, :], scores, -1e30)
    top_score = jnp.max(scores, axis=-1, keepdims=True)
    raised = jnp.exp(scores - top_score)
    probs = (raised / jnp.sum(raised, axis=-1, keepdims=True)).astype(jnp.bfloat16)
    attn = (
        jnp.einsum("hqk,khd->qhd", probs, values, preferred_element_type=jnp.float32)
        .astype(jnp.bfloat16)
        .reshape(slot_count, local_width)
    )
    attn_out = lax.psum_scatter(
        jnp.dot(attn, w_out, preferred_element_type=jnp.float32).astype(jnp.bfloat16),
        "exp",
        scatter_dimension=0,
        tiled=True,
    ).astype(jnp.float32)
    hidden_state = (tokens.astype(jnp.float32) + attn_out).astype(jnp.bfloat16)
    normed2 = norm_rows(hidden_state, moe_gain).astype(jnp.bfloat16)
    top_count = routes.shape[1]
    experts = req_count * exp_count // 2
    capacity = 2 * max(1, rows_dev * top_count * 9 // (16 * experts))
    flat = routes.reshape(-1)
    onehot = (flat[:, None] == jnp.arange(experts, dtype=jnp.int32)[None, :]).astype(jnp.int32)
    slot = jnp.sum((jnp.cumsum(onehot, axis=0) - 1) * onehot, axis=1)
    source_row = jnp.arange(rows_dev * top_count, dtype=jnp.int32) // top_count
    buffer = (
        jnp.zeros((experts, capacity, width), jnp.bfloat16).at[flat, slot].set(normed2[source_row])
    )
    doubled = jnp.broadcast_to(buffer[:, None], (experts, 2, capacity, width)).reshape(
        2 * experts, capacity, width
    )
    rows_in = lax.all_to_all(doubled, ("req", "exp"), split_axis=0, concat_axis=0, tiled=True)
    senders, count, _ = rows_in.shape
    joined_rows = rows_in.reshape(senders * count, width)
    gate = jnp.dot(joined_rows, w_gate[0], preferred_element_type=jnp.float32)
    upper = jnp.dot(joined_rows, w_up[0], preferred_element_type=jnp.float32)
    act = (jax.nn.silu(gate) * upper).astype(jnp.bfloat16)
    part = jnp.dot(act, w_down[0], preferred_element_type=jnp.float32)
    returned = lax.all_to_all(
        part.reshape(senders, count, width).astype(jnp.bfloat16),
        ("req", "exp"),
        split_axis=0,
        concat_axis=0,
        tiled=True,
    ).astype(jnp.float32)
    combined = (
        jnp.sum(returned.reshape(experts, 2, capacity, width), axis=1)
        .astype(jnp.bfloat16)
        .astype(jnp.float32)
    )
    picked = combined[flat, slot].reshape(rows_dev, top_count, width)
    moe = jnp.sum(picked * route_weights[:, :, None], axis=1)
    place = exp_index * rows_dev + jnp.arange(rows_dev, dtype=jnp.int32)
    live_rows = place < length
    return jnp.where(live_rows[:, None], hidden_state.astype(jnp.float32) + moe, 0.0).astype(
        jnp.bfloat16
    )


def solution(mesh):
    return jax.shard_map(
        on_device,
        mesh=mesh,
        in_specs=(
            P(("req", "exp"), None),
            P(),
            P(None, "exp"),
            P(None, "exp"),
            P(None, "exp"),
            P("exp", None),
            P(None, "req", None, "exp"),
            P(),
            P(),
            P(),
            P(("req", "exp"), None, None),
            P(("req", "exp"), None, None),
            P(("req", "exp"), None, None),
            P(("req", "exp"), None),
            P(("req", "exp"), None),
        ),
        out_specs=P(("req", "exp"), None),
        check_vma=False,
    )
```

profile of v0, /device:TPU:9, one launch (start us, length us, event | category | flops | bytes accessed | tf_op | source)
XLA Modules:
  0.0 687.1 jit_solution(17716590146460561715)
XLA Ops:
  11.3 7.0 %gather_fusion = bf16[8,128,2,512]{3,2,1,0:T(2,128)(2,1)} fusion(bf16[4,128,2,512]{3,2,1,0:T(2,128)(2,1)} %param.21, s32[1024]{0:T(1024)S(1)} %pad_clamp_fusion), kind=kCustom, calls=%fused_computation | custom fusion | bytes 4194336 | tf_op jit(solution)/shard_map/jit(_take)/gather | solution.py:71
  18.3 4.9 broadcast_select_fusion
  23.3 4.9 all-to-all-start
  31.5 19.8 %all-to-all-done = bf16[8,128,2,512]{3,2,1,0:T(2,128)(2,1)} async-done(((bf16[8,128,2,512]{3,2,1,0:T(2,128)(2,1)}), bf16[8,128,2,512]{3,2,1,0:T(2,128)(2,1)}, u32[]{:S(2)}, u32[]{:S(2)}) %all-to-all-start) | async-done | bytes 2097184 | tf_op jit(solution)/shard_map/all_to_all | solution.py:72
  51.3 6.7 fusion.54
  58.1 5.8 copy.40
  63.9 4.6 copy.43
  69.8 6.9 %fusion.3 = f32[512,1536]{1,0:T(8,128)S(1)} fusion(bf16[512,2048]{1,0:T(8,128)(2,1)} %all-gather.2.cloned.1.call-done, bf16[2048,512]{1,0:T(8,128)(2,1)} %param.19, bf16[2048,512]{1,0:T(8,128)(2,1)} %param.18, bf16[2048,512]{1,0:T(8,128)(2,1)} %param.17), kind=kOutput, calls=%fused_computation.12 | convolution fusion | flops 3240099840 | bytes 11534336 | tf_op jit(solution)/shard_map/dot_general | solution.py:60
  91.2 7.2 %fusion.57 = (f32[4,512]{1,0:T(4,128)S(1)}, f32[4,512,1536]{2,1,0:T(8,128)}) fusion(f32[4,512,1536]{2,1,0:T(8,128)S(1)} %fusion.24, pred[1536]{0:T(1024)(128)(4,1)S(1)} %concatenate.28), kind=kOutput, calls=%fused_computation.107 | output fusion | flops 18875904 | bytes 25175552 | tf_op jit(solution)/shard_map/sub | solution.py:98
  98.5 7.1 %fusion.30 = bf16[4,128,512]{2,1,0:T(8,128)(2,1)S(1)} fusion(f32[4,512,1536]{2,1,0:T(8,128)} %get-tuple-element.25, f32[4,512]{1,0:T(4,128)S(1)} %get-tuple-element.24, bf16[512,4,128]{0,2,1:T(8,128)(2,1)S(1)} %bitcast.59, bf16[1024,4,128]{0,2,1:T(8,128)(2,1)S(1)} %bitcast.58), kind=kOutput, calls=%fused_computation.49 | convolution fusion | flops 815005696 | bytes 14688256 | tf_op jit(solution)/shard_map/hqk,khd->qhd/dot_general | solution.py:101
  108.7 4.5 reduce-window.6
  113.9 38.4 %reduce-scatter.2.cloned.1.call-done = bf16[128,2048]{1,0:T(8,128)(2,1)} async-done(((bf16[512,2048]{1,0:T(8,128)(2,1)}), bf16[128,2048]{1,0:T(8,128)(2,1)}) %reduce-scatter.2.cloned.1.call-update) | async-done | bytes 524304 | tf_op jit(solution)/shard_map/reduce_scatter | solution.py:105
  154.9 23.1 %scatter_custom_fusion = bf16[1152,2048]{1,0:T(8,128)(2,1)} fusion(s32[1024]{0:T(1024)S(1)} %get-tuple-element.29, bf16[128,2048]{1,0:T(8,128)(2,1)S(1)} %fusion.39, s32[1024]{0:T(1024)S(1)} %get-tuple-element.28, bf16[]{:T(256)} %constant.81.clone.1), kind=kCustom, calls=%fused_computation.25 | custom fusion | bytes 4718594
  178.0 7.5 %broadcast_in_dim.43 = bf16[16,2,72,2048]{3,2,1,0:T(8,128)(2,1)} broadcast(bf16[16,72,2048]{2,1,0:T(8,128)(2,1)} %bitcast.54), dimensions={0,2,3} | broadcast | bytes 14155776 | tf_op jit(solution)/shard_map/broadcast_in_dim | solution.py:123
  185.5 211.2 %all_to_all.19 = bf16[32,72,2048]{2,1,0:T(8,128)(2,1)S(1)} all-to-all(bf16[32,72,2048]{2,1,0:T(8,128)(2,1)} %bitcast.53), channel_id=1, replica_groups=mesh['req'=8,'exp'=4] {'req','exp'}, dimensions={0} | all-to-all | bytes 18874368 | tf_op jit(solution)/shard_map/all_to_all | solution.py:126
  396.7 5.1 fusion.19
  401.8 6.1 fusion.13
  407.9 7.4 %convolution_convert_fusion = bf16[32,72,2048]{2,1,0:T(8,128)(2,1)} fusion(bf16[32,72,512]{2,1,0:T(8,128)(2,1)S(1)} %bitcast.64, bf16[1,512,2048]{2,1,0:T(8,128)(2,1)S(1)} %copy-done), kind=kOutput, calls=%fused_computation.22 | convolution fusion | flops 4836556800 | bytes 13893632 | tf_op jit(solution)/shard_map/dot_general | solution.py:132
  415.3 5.3 all-to-all-start.2
  421.3 208.2 %all-to-all-done.2 = bf16[32,72,2048]{2,1,0:T(8,128)(2,1)} async-done(((bf16[32,72,2048]{2,1,0:T(8,128)(2,1)}), bf16[32,72,2048]{2,1,0:T(8,128)(2,1)}, u32[]{:S(2)}, u32[]{:S(2)}) %all-to-all-start.2) | async-done | bytes 9437216 | tf_op jit(solution)/shard_map/all_to_all | solution.py:133
  629.6 9.9 %bitcast_reduce_fusion = bf16[16,72,2048]{2,1,0:T(8,128)(2,1)} fusion(bf16[32,72,2048]{2,1,0:T(8,128)(2,1)} %all-to-all-done.2), kind=kLoop, calls=%fused_computation.9 | loop fusion | flops 2359296 | bytes 14155776 | tf_op jit(solution)/shard_map/reduce_sum | solution.py:141
  639.4 7.2 %convert_element_type.90 = f32[16,72,2048]{2,1,0:T(8,128)} convert(bf16[16,72,2048]{2,1,0:T(8,128)(2,1)} %bitcast_reduce_fusion) | non-fusion elementwise | flops 2359296 | bytes 14155776 | tf_op jit(solution)/shard_map/convert_element_type | solution.py:143
  646.6 25.8 %gather_fusion.1 = f32[1024,2048]{1,0:T(8,128)} fusion(f32[16,72,2048]{2,1,0:T(8,128)} %convert_element_type.90, s32[1024]{0:T(1024)S(1)} %bitcast.52), kind=kCustom, calls=%fused_computation.2 | custom fusion | bytes 16785408 | tf_op jit(solution)/shard_map/gather | solution.py:145
  672.4 6.6 fusion.2
  (82 shorter events, 32.0 us)
Async XLA Ops:
  6.5 401.4 %copy-start = (bf16[1,512,2048]{2,1,0:T(8,128)(2,1)S(1)}, bf16[1,512,2048]{2,1,0:T(8,128)(2,1)}, u32[]{:S(2)}) copy-start(bf16[1,512,2048]{2,1,0:T(8,128)(2,1)} %param.27) | copy-start | bytes 6291460
  6.5 63.3 %all-gather.2.cloned.1.call-start = ((), (), s32[]{:S(2)}) async-start(), calls=%async_computation.4 | async-start | bytes 2621440 | tf_op jit(solution)/shard_map/all_gather | solution.py:58
  18.3 10.1 %copy-start.15 = (s32[8]{0:T(128)S(1)}, s32[8]{0:T(128)}, u32[]{:S(2)}) copy-start(s32[8]{0:T(128)} %param.23) | copy-start | bytes 100
  23.3 28.1 %all-to-all-start = ((bf16[8,128,2,512]{3,2,1,0:T(2,128)(2,1)}), bf16[8,128,2,512]{3,2,1,0:T(2,128)(2,1)}, u32[]{:S(2)}, u32[]{:S(2)}) async-start(bf16[8,128,2,512]{3,2,1,0:T(2,128)(2,1)} %broadcast_select_fusion), calls=%async_computation | async-start | bytes 4194304 | tf_op jit(solution)/shard_map/all_to_all | solution.py:72
  28.2 124.1 %reduce-scatter.2.cloned.1.call-start = ((), (), s32[]{:S(2)}) async-start(), calls=%async_computation.5 | async-start | bytes 2621440 | tf_op jit(solution)/shard_map/reduce_scatter | solution.py:105
  85.3 2.9 copy-start.5
  88.1 1.2 copy-start.3
  91.2 7.2 %copy-start.4 = (bf16[1024,1,512]{0,2,1:T(8,128)(2,1)S(1)}, bf16[1024,1,512]{0,2,1:T(8,128)(2,1)}, u32[]{:S(2)}) copy-start(bf16[1024,1,512]{0,2,1:T(8,128)(2,1)} %copy.40) | copy-start | bytes 3145732
  91.2 7.2 %copy-start.6 = (bf16[512,512]{0,1:T(8,128)(2,1)S(1)}, bf16[512,512]{0,1:T(8,128)(2,1)}, u32[]{:S(2)}) copy-start(bf16[512,512]{0,1:T(8,128)(2,1)} %copy.39) | copy-start | bytes 1572868
  98.5 7.1 %copy-start.12 = (bf16[512,2048]{1,0:T(8,128)(2,1)S(1)}, bf16[512,2048]{1,0:T(8,128)(2,1)}, u32[]{:S(2)}) copy-start(bf16[512,2048]{1,0:T(8,128)(2,1)} %param.20) | copy-start | bytes 6291460
  105.5 2.7 copy-start.8
  105.6 8.1 %copy-start.11 = (s32[2]{0:T(128)S(1)}, s32[2]{0:T(128)}, u32[]{:S(2)}) copy-start(s32[2]{0:T(128)} %constant.93) | copy-start | bytes 28
  105.6 8.2 %copy-start.10 = (s32[2]{0:T(128)S(1)}, s32[2]{0:T(128)}, u32[]{:S(2)}) copy-start(s32[2]{0:T(128)} %constant.96) | copy-start | bytes 28
  105.6 46.7 %copy-start.1 = (bf16[128,2048]{1,0:T(8,128)(2,1)S(1)}, bf16[128,2048]{1,0:T(8,128)(2,1)}, u32[]{:S(2)}) copy-start(bf16[128,2048]{1,0:T(8,128)(2,1)} %param.15) | copy-start | bytes 1572868
  105.6 48.0 %copy-start.7 = (f32[2048]{0:T(1024)S(1)}, f32[2048]{0:T(1024)}, u32[]{:S(2)}) copy-start(f32[2048]{0:T(1024)} %param.24) | copy-start | bytes 24580
  185.5 211.2 %copy-start.13 = (bf16[1,2048,512]{2,1,0:T(8,128)(2,1)S(1)}, bf16[1,2048,512]{2,1,0:T(8,128)(2,1)}, u32[]{:S(2)}) copy-start(bf16[1,2048,512]{2,1,0:T(8,128)(2,1)} %param.25) | copy-start | bytes 6291460
  396.7 5.1 copy-start.14
  415.3 5.3 copy-start.9
  415.3 214.3 %all-to-all-start.2 = ((bf16[32,72,2048]{2,1,0:T(8,128)(2,1)}), bf16[32,72,2048]{2,1,0:T(8,128)(2,1)}, u32[]{:S(2)}, u32[]{:S(2)}) async-start(bf16[32,72,2048]{2,1,0:T(8,128)(2,1)} %convolution_convert_fusion), calls=%async_computation.3 | async-start | bytes 18874368 | tf_op jit(solution)/shard_map/all_to_all | solution.py:133
  672.4 6.6 copy-start.2
Sparse Core Ops, SparseCore 0:
  10.1 45.2 all-gather.1
  108.4 43.8 reduce-scatter.1
where the time goes:
time: 693 us; the launch traced here: 687 us
  waiting for transfers between devices  266 us (38%)
  blocking collectives  211 us (30%)
  local copies, waits for them, and re-layouts  95.4 us (14%)
  other arithmetic  52.6 us (8%)
  matrix products  37 us (5%)
  between operations  14 us (2%)
  starting transfers between devices  10.4 us (2%)
    all_to_all x1, blocking collectives, on_device(): lax.all_to_all(doubled, ('req', 'exp'), split_axis=0, concat_axis=0, tile...  211 us
    all_to_all x1, waiting for transfers between devices, on_device(): lax.all_to_all(part.reshape(senders, count, width).astype(jnp.bfloat16),...  208 us
    reduce_scatter x1, waiting for transfers between devices, on_device(): lax.psum_scatter(jnp.dot(attn, w_out, preferred_element_type=jnp.float32)...  38.4 us
    unnamed x37, local copies, waits for them, and re-layouts  34.4 us
    gather x1, local copies, waits for them, and re-layouts, on_device(): picked = combined[flat, slot].reshape(rows_dev, top_count, width)  25.8 us
    all_to_all x1, waiting for transfers between devices, on_device(): lax.all_to_all(outgoing, 'req', split_axis=0, concat_axis=1, tiled=True)[0]  19.8 us
  transfers between devices with their start and end apart: 4, of which 3 were waited for; matrix products, arithmetic and copies ran while one was open for 6% of the time, Pallas kernels for 0%

commit v1 on v0

v1 whole, which is shorter than its diff:
```python
import functools
import math

import jax
import jax.numpy as jnp
from jax import lax
from jax.experimental import pallas as pl
from jax.experimental.pallas import tpu as pltpu
from jax.sharding import PartitionSpec as P

HD = 128
PREFIX = 1024
MESH = pl.DeviceIdType.MESH
ANY = pl.BlockSpec(memory_space=pl.ANY)
BOTH = ("req", "exp")


def norm_rows(values, gain):
    wide = values.astype(jnp.float32)
    return wide * lax.rsqrt(jnp.mean(wide * wide, axis=-1, keepdims=True) + 1e-05) * gain


def greet(peers):
    barrier = pltpu.get_barrier_semaphore()
    for peer in peers:
        pl.semaphore_signal(barrier, inc=1, device_id=peer, device_id_type=MESH)
    pl.semaphore_wait(barrier, len(peers))


def remote(src, dst, sems, i, peer):
    return pltpu.make_async_remote_copy(
        src_ref=src,
        dst_ref=dst,
        send_sem=sems.at[0, i],
        recv_sem=sems.at[1, i],
        device_id=peer,
        device_id_type=MESH,
    )


def plane():
    q = lax.axis_index("req")
    z = lax.axis_index("exp")
    core = lax.rem(q, 2)
    x = lax.rem(q // 2, 2)
    y = q // 4
    xn = q + 2 - 4 * x
    yn = q + 4 - 8 * y
    dg = xn + 4 - 8 * y
    other = 1 - 2 * core
    return q, z, xn, yn, dg, other


def first_kernel(nz, nq, tok, pre, tok_out, pre_out, zs, qs, ls):
    q = lax.axis_index("req")
    z = lax.axis_index("exp")
    zp = [(q, lax.rem(z + j, nz)) for j in range(1, nz)]
    qp = [lax.rem(q + j, nq) for j in range(1, nq)]
    greet(zp + [(p, z) for p in qp])
    copies = []
    for i, peer in enumerate(zp):
        c = remote(tok, tok_out.at[z], zs, i, peer)
        c.start()
        copies.append(c)
    for i, p in enumerate(qp):
        c = remote(pre.at[p], pre_out.at[q], qs, i, (p, z))
        c.start()
        copies.append(c)
    for c in (
        pltpu.make_async_copy(tok, tok_out.at[z], ls.at[0]),
        pltpu.make_async_copy(pre.at[q], pre_out.at[q], ls.at[1]),
    ):
        c.start()
        copies.append(c)
    for c in copies:
        c.wait()


def first(tokens, outgoing, nz, nq):
    return pl.pallas_call(
        functools.partial(first_kernel, nz, nq),
        out_shape=(
            jax.ShapeDtypeStruct((nz,) + tokens.shape, tokens.dtype),
            jax.ShapeDtypeStruct(outgoing.shape, outgoing.dtype),
        ),
        in_specs=[ANY, ANY],
        out_specs=(ANY, ANY),
        scratch_shapes=[
            pltpu.SemaphoreType.DMA((2, nz - 1)),
            pltpu.SemaphoreType.DMA((2, nq - 1)),
            pltpu.SemaphoreType.DMA((2,)),
        ],
        compiler_params=pltpu.CompilerParams(collective_id=0, has_side_effects=True),
    )(tokens, outgoing)


def heads_kernel(nz, width, src, dst, zs, ls):
    q = lax.axis_index("req")
    z = lax.axis_index("exp")
    peers = [(q, lax.rem(z + j, nz)) for j in range(1, nz)]
    greet(peers)
    mine = dst.at[:, pl.ds(pl.multiple_of(z * width, width), width)]
    copies = [remote(src, mine, zs, i, peer) for i, peer in enumerate(peers)]
    copies.append(pltpu.make_async_copy(src, mine, ls))
    for c in copies:
        c.start()
    for c in copies:
        c.wait()


def heads(attn, nz):
    rows, width = attn.shape
    return pl.pallas_call(
        functools.partial(heads_kernel, nz, width),
        out_shape=jax.ShapeDtypeStruct((rows, nz * width), attn.dtype),
        in_specs=[ANY],
        out_specs=ANY,
        scratch_shapes=[pltpu.SemaphoreType.DMA((2, nz - 1)), pltpu.SemaphoreType.DMA],
        compiler_params=pltpu.CompilerParams(collective_id=1, has_side_effects=True),
    )(attn)


def attend_kernel(length, tok, gain, wq, wk, wv, cosine, sine, pk, pv, out, normed):
    @pl.when(pl.program_id(0) == 0)
    def _():
        normed[...] = norm_rows(tok[...], gain[...]).astype(jnp.bfloat16)

    def project(w):
        return jnp.dot(normed[...], w[...], preferred_element_type=jnp.float32)

    def rot(v):
        return (v * cosine[...] + pltpu.roll(v, HD // 2, 1) * sine[...]).astype(jnp.bfloat16)

    def across(a, b):
        return lax.dot_general(a, b, (((1,), (1,)), ((), ())), preferred_element_type=jnp.float32)

    query = rot(project(wq))
    key = rot(project(wk))
    value = project(wv).astype(jnp.bfloat16)
    scale = 1.0 / math.sqrt(HD)
    s1 = across(query, pk[...]) * scale
    s2 = across(query, key) * scale
    live = lax.broadcasted_iota(jnp.int32, s2.shape, 1) < length[0]
    s2 = jnp.where(live, s2, -1e30)
    top = jnp.maximum(
        jnp.max(s1, axis=-1, keepdims=True), jnp.max(s2, axis=-1, keepdims=True)
    )
    e1 = jnp.exp(s1 - top)
    e2 = jnp.exp(s2 - top)
    total = jnp.sum(e1, axis=-1, keepdims=True) + jnp.sum(e2, axis=-1, keepdims=True)
    inv = 1.0 / total
    p1 = (e1 * inv).astype(jnp.bfloat16)
    p2 = (e2 * inv).astype(jnp.bfloat16)
    attn = jnp.dot(p1, pv[...], preferred_element_type=jnp.float32)
    attn += jnp.dot(p2, value, preferred_element_type=jnp.float32)
    out[...] = attn.astype(jnp.bfloat16)


def attend(length, tok, gain, wq, wk, wv, cosine, sine, prefix):
    rows, width = tok.shape
    local = wq.shape[1]
    n = local // HD
    whole = lambda a: pl.BlockSpec(a.shape, lambda h, s: (0, 0))
    weight = pl.BlockSpec((width, HD), lambda h, s: (0, h))
    return pl.pallas_call(
        attend_kernel,
        out_shape=jax.ShapeDtypeStruct((rows, local), jnp.bfloat16),
        grid_spec=pltpu.PrefetchScalarGridSpec(
            num_scalar_prefetch=1,
            grid=(n,),
            in_specs=[
                whole(tok),
                whole(gain),
                weight,
                weight,
                weight,
                whole(cosine),
                whole(sine),
                pl.BlockSpec((prefix.shape[0], HD), lambda h, s: (0, h)),
                pl.BlockSpec((prefix.shape[0], HD), lambda h, s: (0, n + h)),
            ],
            out_specs=pl.BlockSpec((rows, HD), lambda h, s: (0, h)),
            scratch_shapes=[pltpu.VMEM((rows, width), jnp.bfloat16)],
        ),
        compiler_params=pltpu.CompilerParams(vmem_limit_bytes=56 * 2**20),
    )(length, tok, gain, wq, wk, wv, cosine, sine, prefix, prefix)


def gather_kernel(src, out, sems, ls):
    q, z, xn, yn, dg, other = plane()
    rows = src.shape[0]
    half = rows // 2
    top, low = pl.ds(0, half), pl.ds(half, half)
    tox, toy, sib = (xn, z), (yn, z), (q + other, z)
    greet([tox, toy, sib])
    own = pltpu.make_async_copy(src, out.at[q], ls)
    x1 = remote(src.at[top], out.at[q, top], sems, 0, tox)
    y1 = remote(src.at[low], out.at[q, low], sems, 1, toy)
    x2 = remote(src.at[low], out.at[q, low], sems, 2, tox)
    y2 = remote(src.at[top], out.at[q, top], sems, 3, toy)
    s0 = remote(src, out.at[q], sems, 4, sib)
    for c in (x1, y1, x2, y2, s0, own):
        c.start()
    y3 = remote(out.at[xn, top], out.at[xn, top], sems, 5, toy)
    x3 = remote(out.at[yn, low], out.at[yn, low], sems, 6, tox)
    hand = [
        remote(out.at[r, part], out.at[r, part], sems, 7 + i, sib)
        for i, (r, part) in enumerate(
            ((xn, top), (yn, low), (xn, low), (yn, top), (dg, top), (dg, low))
        )
    ]
    x1.wait_recv()
    y3.start()
    hand[0].start()
    y1.wait_recv()
    x3.start()
    hand[1].start()
    x2.wait_recv()
    hand[2].start()
    y2.wait_recv()
    hand[3].start()
    y3.wait_recv()
    hand[4].start()
    x3.wait_recv()
    hand[5].start()
    for c in (x1, y1, x2, y2, y3, x3):
        c.wait_send()
    for c in [s0, own] + hand:
        c.wait()


def gather(rows_of, nq):
    return pl.pallas_call(
        gather_kernel,
        out_shape=jax.ShapeDtypeStruct((nq,) + rows_of.shape, rows_of.dtype),
        in_specs=[ANY],
        out_specs=ANY,
        scratch_shapes=[pltpu.SemaphoreType.DMA((2, 13)), pltpu.SemaphoreType.DMA],
        compiler_params=pltpu.CompilerParams(collective_id=2, has_side_effects=True),
    )(rows_of)


def expert_kernel(lengths, x, w, gate, up, down, out):
    rows = x.shape[0]
    start = pl.program_id(1) * rows
    live = start < lengths[pl.program_id(0)]

    @pl.when(live)
    def _():
        g = jnp.dot(x[...], gate[...], preferred_element_type=jnp.float32)
        u = jnp.dot(x[...], up[...], preferred_element_type=jnp.float32)
        act = (g / (1.0 + jnp.exp(-g)) * u).astype(jnp.bfloat16)
        part = jnp.dot(act, down[...], preferred_element_type=jnp.float32)
        out[...] = (part * w[...]).astype(jnp.bfloat16)

    @pl.when(jnp.logical_not(live))
    def _():
        out[...] = jnp.zeros_like(out)


def experts_on(lengths, x, w, gate, up, down, slots):
    count, width = x.shape
    block = 256
    per = slots // block
    fixed = lambda a: pl.BlockSpec(a.shape, lambda r, b, s: (0, 0))
    rows = lambda c: pl.BlockSpec((block, c), lambda r, b, s: (r * per + b, 0))
    return pl.pallas_call(
        expert_kernel,
        out_shape=jax.ShapeDtypeStruct((count, width), jnp.bfloat16),
        grid_spec=pltpu.PrefetchScalarGridSpec(
            num_scalar_prefetch=1,
            grid=(count // slots, per),
            in_specs=[rows(width), rows(1), fixed(gate), fixed(up), fixed(down)],
            out_specs=rows(width),
        ),
        compiler_params=pltpu.CompilerParams(vmem_limit_bytes=56 * 2**20),
    )(lengths, x, w, gate, up, down)


def scatter_kernel(nz, parts, out, held, came, rx, ry, rz, sems, zs, ls):
    q, z, xn, yn, dg, other = plane()
    slots, width = parts.shape[1:]
    half = width // 2
    mine_rows = slots // nz
    left, right = pl.ds(0, half), pl.ds(half, half)
    tox, toy, sib = (xn, z), (yn, z), (q + other, z)
    peers = [lax.rem(z + j, nz) for j in range(1, nz)]
    greet([tox, toy, sib] + [(q, p) for p in peers])
    order = (dg, xn, yn, q)
    DG, XN, YN, ME = range(4)
    swap = [remote(parts.at[r + other], came.at[k], sems, k, sib) for k, r in enumerate(order)]
    load = [pltpu.make_async_copy(parts.at[r], held.at[k], ls.at[k]) for k, r in enumerate(order)]
    for c in swap:
        c.start()
    for c in load:
        c.start()
    step = 64

    def add(dst, src):
        @pl.loop(0, slots // step)
        def _(i):
            at = pl.ds(pl.multiple_of(i * step, step), step)
            dst[at, :] = dst[at, :] + src[at, :]

    x1 = remote(held.at[DG, :, left], rx.at[0], sems, 4, tox)
    y1 = remote(held.at[DG, :, right], ry.at[0], sems, 5, toy)
    x2 = remote(held.at[XN, :, left], rx.at[1], sems, 6, tox)
    y2 = remote(held.at[YN, :, right], ry.at[1], sems, 7, toy)
    x3 = remote(held.at[XN, :, right], rx.at[2], sems, 8, tox)
    y3 = remote(held.at[YN, :, left], ry.at[2], sems, 9, toy)
    for k, after in ((DG, (x1, y1)), (XN, (x2,)), (YN, (y2,)), (ME, ())):
        swap[k].wait_recv()
        load[k].wait()
        add(held.at[k], came.at[k])
        for c in after:
            c.start()
    x1.wait_recv()
    add(held.at[YN, :, left], rx.at[0])
    y3.start()
    y1.wait_recv()
    add(held.at[XN, :, right], ry.at[0])
    x3.start()
    x2.wait_recv()
    add(held.at[ME, :, left], rx.at[1])
    y2.wait_recv()
    add(held.at[ME, :, right], ry.at[1])

    def shard(p, cols):
        return held.at[ME, pl.ds(pl.multiple_of(p * mine_rows, mine_rows), mine_rows), cols]

    sent = []
    for side, cols, c, came_in in ((0, left, y3, ry.at[2]), (1, right, x3, rx.at[2])):
        c.wait_recv()
        add(held.at[ME, :, cols], came_in)
        for i, p in enumerate(peers):
            s = remote(shard(p, cols), rz.at[i, :, cols], zs, side * (nz - 1) + i, (q, p))
            s.start()
            sent.append(s)
    own = shard(z, slice(None))
    for s in sent:
        s.wait()
    total = own[...].astype(jnp.float32)
    for i in range(nz - 1):
        total += rz[i].astype(jnp.float32)
    out[...] = total
    for c in swap + [x1, y1, x2, y2, x3, y3]:
        c.wait_send()


def scatter(parts, nz):
    nq, slots, width = parts.shape
    bf = jnp.bfloat16
    return pl.pallas_call(
        functools.partial(scatter_kernel, nz),
        out_shape=jax.ShapeDtypeStruct((slots // nz, width), jnp.float32),
        in_specs=[ANY],
        out_specs=pl.BlockSpec(memory_space=pltpu.VMEM),
        scratch_shapes=[
            pltpu.VMEM((4, slots, width), bf),
            pltpu.VMEM((4, slots, width), bf),
            pltpu.VMEM((3, slots, width // 2), bf),
            pltpu.VMEM((3, slots, width // 2), bf),
            pltpu.VMEM((nz - 1, slots // nz, width), bf),
            pltpu.SemaphoreType.DMA((2, 10)),
            pltpu.SemaphoreType.DMA((2, 2 * (nz - 1))),
            pltpu.SemaphoreType.DMA((4,)),
        ],
        compiler_params=pltpu.CompilerParams(
            collective_id=3, has_side_effects=True, vmem_limit_bytes=56 * 2**20
        ),
    )(parts)


def on_device(
    tokens,
    attn_gain,
    w_query,
    w_key,
    w_value,
    w_out,
    prefix_cache,
    group_of,
    lengths,
    moe_gain,
    w_gate,
    w_up,
    w_down,
    routes,
    route_weights,
):
    rows_dev, width = tokens.shape
    nz = lax.axis_size("exp")
    nq = lax.axis_size("req")
    z = lax.axis_index("exp")
    q = lax.axis_index("req")
    paths = (nq, nz) == (8, 4)
    local = w_query.shape[1]
    slots = rows_dev * nz
    experts = nq * nz // 2

    groups, piece, _, _ = prefix_cache.shape
    flat_cache = prefix_cache.reshape(groups, piece, 2 * local)
    outgoing = jnp.stack(
        [lax.dynamic_index_in_dim(flat_cache, group_of[r], 0, keepdims=False) for r in range(nq)]
    )
    if paths:
        mine, arrived = first(tokens, outgoing, nz, nq)
    else:
        mine = lax.all_gather(tokens, "exp", axis=0)
        arrived = lax.all_to_all(outgoing, "req", split_axis=0, concat_axis=0, tiled=True)
    mine = mine.reshape(slots, width)
    arrived = arrived.reshape(nq * piece, 2 * local)

    share = w_out.shape[0] // nq
    w_part = lax.dynamic_slice_in_dim(w_out, q * share, share, 0)
    w_whole = lax.all_gather(w_part, ("exp", "req"), axis=0, tiled=True)

    named = routes[:, :, None] == jnp.arange(experts, dtype=jnp.int32)
    dense = jnp.sum(jnp.where(named, route_weights[:, :, None], 0.0), axis=1)
    dense = lax.all_gather(dense, BOTH, axis=0, tiled=True)
    expert = (q * nz + z) // 2
    weight = jnp.sum(
        jnp.where(jnp.arange(experts, dtype=jnp.int32) == expert, dense, 0.0), axis=1, keepdims=True
    )

    half = HD // 2
    freqs = 10000.0 ** (-(jnp.arange(half, dtype=jnp.float32) * 2.0) / HD)
    places = (PREFIX + jnp.arange(slots, dtype=jnp.int32)).astype(jnp.float32)
    angles = places[:, None] * freqs[None, :]
    cosine = jnp.cos(angles)
    sine = jnp.sin(angles)
    cosine = jnp.concatenate([cosine, cosine], axis=1)
    sine = jnp.concatenate([-sine, sine], axis=1)

    length = lax.dynamic_slice_in_dim(lengths, q, 1, 0)
    attn = attend(
        length, mine, attn_gain[None, :], w_query, w_key, w_value, cosine, sine, arrived
    )
    attn = heads(attn, nz) if paths else lax.all_gather(attn, "exp", axis=1, tiled=True)
    attn_out = jnp.dot(attn, w_whole, preferred_element_type=jnp.float32)
    hidden = (mine.astype(jnp.float32) + attn_out).astype(jnp.bfloat16)
    normed2 = norm_rows(hidden, moe_gain).astype(jnp.bfloat16)
    if paths:
        every = gather(normed2, nq).reshape(nq * slots, width)
    else:
        every = lax.all_gather(normed2, "req", axis=0, tiled=True)
    parts = experts_on(lengths, every, weight, w_gate[0], w_up[0], w_down[0], slots)
    if paths:
        moe = scatter(parts.reshape(nq, slots, width), nz)
    else:
        moe = lax.psum_scatter(parts, "req", scatter_dimension=0, tiled=True)
        moe = lax.psum_scatter(moe, "exp", scatter_dimension=0, tiled=True).astype(jnp.float32)
    own = lax.dynamic_slice_in_dim(hidden, z * rows_dev, rows_dev, 0)
    place = z * rows_dev + jnp.arange(rows_dev, dtype=jnp.int32)
    return jnp.where((place < length)[:, None], own.astype(jnp.float32) + moe, 0.0).astype(
        jnp.bfloat16
    )


def solution(mesh):
    spread = P(BOTH, None, None)
    return jax.shard_map(
        on_device,
        mesh=mesh,
        in_specs=(
            P(BOTH, None),
            P(),
            P(None, "exp"),
            P(None, "exp"),
            P(None, "exp"),
            P("exp", None),
            P(None, "req", None, "exp"),
            P(),
            P(),
            P(),
            spread,
            spread,
            spread,
            P(BOTH, None),
            P(BOTH, None),
        ),
        out_specs=P(BOTH, None),
        check_vma=False,
    )
```

time: 693 us -> 479 us (0.69)
  Pallas kernels: 0 us -> 357 us
  waiting for transfers between devices: 266 us -> 0.04 us
  blocking collectives: 211 us -> 62.2 us
  local copies, waits for them, and re-layouts: 95.4 us -> 14.2 us
  other arithmetic: 52.6 us -> 6.98 us
  matrix products: 37 us -> 9.27 us
  between operations: 14 us -> 29 us
  starting transfers between devices: 10.4 us -> 0.01 us
    pallas_call x0 -> x6, Pallas kernels: none -> 357 us  [the longest x1 123 us: scatter(): pl.pallas_call(functools.partial(scatter_kernel, nz), out_shape=jax.Shape...]
    all_to_all x2 -> x0, waiting for transfers between devices: 228 us -> none  [the longest x1 208 us: on_device(): lax.all_to_all(part.reshape(senders, count, width).astype(jnp.bfloat16),...]
    all_to_all x1 -> x0, blocking collectives: 211 us -> none  [on_device(): lax.all_to_all(doubled, ('req', 'exp'), split_axis=0, concat_axis=0, tile...]
    all_gather x0 -> x1, blocking collectives: none -> 62.2 us  [on_device(): dense = lax.all_gather(dense, BOTH, axis=0, tiled=True)]
    reduce_scatter x1 -> x0, waiting for transfers between devices: 38.4 us -> none  [on_device(): lax.psum_scatter(jnp.dot(attn, w_out, preferred_element_type=jnp.float32)...]
    gather x2 -> x0, local copies, waits for them, and re-layouts: 32.8 us -> none  [the longest x1 25.8 us: on_device(): picked = combined[flat, slot].reshape(rows_dev, top_count, width)]
    dot_general x7 -> x1, matrix products: 37 us -> 9.27 us  [on_device(): attn_out = jnp.dot(attn, w_whole, preferred_element_type=jnp.float32)]
    unnamed x37 -> x21, local copies, waits for them, and re-layouts: 34.4 us -> 6.7 us
  transfers between devices with their start and end apart: 4 -> 1, of which waited for: 3 -> 0; matrix products, arithmetic and copies ran while one was open for 6% -> 3% of each run, Pallas kernels for 0% -> 25%
where the time goes in v1:
time: 479 us; the launch traced here: 478 us
  Pallas kernels  357 us (75%)
  blocking collectives  62.2 us (13%)
  between operations  29 us (6%)
  local copies, waits for them, and re-layouts  14.2 us (3%)
  matrix products  9.27 us (2%)
  other arithmetic  6.98 us (1%)
    pallas_call x1, Pallas kernels, scatter(): pl.pallas_call(functools.partial(scatter_kernel, nz), out_shape=jax.Shape...  123 us
    pallas_call x1, Pallas kernels, gather(): pl.pallas_call(gather_kernel, out_shape=jax.ShapeDtypeStruct((nq,) + rows...  76.6 us
    all_gather x1, blocking collectives, on_device(): dense = lax.all_gather(dense, BOTH, axis=0, tiled=True)  62.2 us
    pallas_call x1, Pallas kernels, first(): pl.pallas_call(functools.partial(first_kernel, nz, nq), out_shape=(jax.Sh...  54.3 us
    pallas_call x1, Pallas kernels, heads(): pl.pallas_call(functools.partial(heads_kernel, nz, width), out_shape=jax....  47.1 us
    pallas_call x1, Pallas kernels, experts_on(): pl.pallas_call(expert_kernel, out_shape=jax.ShapeDtypeStruct((count, widt...  35.8 us
    pallas_call x1, Pallas kernels, attend(): pl.pallas_call(attend_kernel, out_shape=jax.ShapeDtypeStruct((rows, local...  20.1 us
  transfers between devices with their start and end apart: 1, of which 0 were waited for; matrix products, arithmetic and copies ran while one was open for 3% of the time, Pallas kernels for 25%

profile of v1, /device:TPU:9, one launch (start us, length us, event | category | flops | bytes accessed | tf_op | source)
XLA Modules:
  0.0 478.5 jit_solution(17387346720679566406)
XLA Ops:
  6.6 1.6 copy-done
  8.1 0.7 constant_dynamic-slice_fusion
  8.9 1.6 fusion.4
  20.8 1.8 reshape.43
  22.7 62.2 %all_gather.7 = f32[4096,16]{0,1:T(8,128)S(1)} all-gather(f32[128,16]{0,1:T(8,128)S(1)} %select_reduce_fusion.1), channel_id=1, replica_groups=mesh['req'=8,'exp'=4] {'req','exp'}, dimensions={0}, use_global_device_ids=true | all-gather | bytes 270336 | tf_op jit(solution)/shard_map/all_gather | solution.py:420
  85.1 2.0 copy.21.w
  92.8 0.7 dynamic-slice_dynamic-update-slice_fusion.7
  93.5 0.7 dynamic-slice_dynamic-update-slice_fusion.6
  94.3 0.7 dynamic-slice_dynamic-update-slice_fusion.5
  95.0 0.7 dynamic-slice_dynamic-update-slice_fusion.4
  95.8 0.7 dynamic-slice_dynamic-update-slice_fusion.3
  96.5 0.7 dynamic-slice_dynamic-update-slice_fusion.2
  97.2 0.7 dynamic-slice_dynamic-update-slice_fusion.1
  98.6 54.3 %shard_map.145 = (bf16[4,128,2048]{2,1,0:T(8,128)(2,1)}, bf16[8,128,1024]{2,1,0:T(8,128)(2,1)}) custom-call(bf16[128,2048]{1,0:T(8,128)(2,1)} %tok.1, bf16[8,128,1024]{2,1,0:T(8,128)(2,1)} %dynamic-slice_dynamic-update-slice_fusion.pre), custom_call_target="tpu_custom_call" | custom-call | tf_op jit(solution)/shard_map/pallas_call | solution.py:80
  152.9 1.0 fusion.3
  153.9 1.0 pad_maximum_fusion
  155.0 20.1 %shard_map.146.src = bf16[512,512]{1,0:T(8,128)(2,1)} custom-call(s32[1]{0:T(128)} %dynamic_slice.34.length, bf16[512,2048]{1,0:T(8,128)(2,1)} %bitcast.27, f32[1,2048]{1,0:T(1,128)} %bitcast.30, bf16[2048,512]{1,0:T(8,128)(2,1)} %wq.1, bf16[2048,512]{1,0:T(8,128)(2,1)} %wk.1, bf16[2048,512]{1,0:T(8,128)(2,1)} %wv.1, f32[512,128]{1,0:T(8,128)} %get-tuple-element.22.cosine, ...), custom_call_target="tpu_custom_call" | custom-call | tf_op jit(solution)/shard_map/pallas_call | solution.py:165
  175.1 47.1 %shard_map.147 = bf16[512,2048]{1,0:T(8,128)(2,1)} custom-call(bf16[512,512]{1,0:T(8,128)(2,1)} %shard_map.146.src), custom_call_target="tpu_custom_call" | custom-call | tf_op jit(solution)/shard_map/pallas_call | solution.py:113
  222.8 9.3 %fusion = (f32[512]{0:T(512)S(1)}, bf16[512,2048]{1,0:T(8,128)(2,1)S(1)}) fusion(bf16[512,2048]{1,0:T(8,128)(2,1)} %shard_map.147, bf16[2048,2048]{1,0:T(8,128)(2,1)} %all-gather.2.cloned.1.call-done, bf16[512,2048]{1,0:T(8,128)(2,1)} %bitcast.28), kind=kOutput, calls=%fused_computation.2 | convolution fusion | flops 4301258240 | bytes 14682112 | tf_op jit(solution)/shard_map/dot_general | solution.py:440
  232.1 2.0 fusion.2.src
  234.1 76.6 %shard_map.148 = bf16[8,512,2048]{2,1,0:T(8,128)(2,1)} custom-call(bf16[512,2048]{1,0:T(8,128)(2,1)} %fusion.2.src), custom_call_target="tpu_custom_call" | custom-call | tf_op jit(solution)/shard_map/pallas_call | solution.py:233
  310.6 35.8 %shard_map.149 = bf16[4096,2048]{1,0:T(8,128)(2,1)} custom-call(s32[8]{0:T(128)} %lengths.1, bf16[4096,2048]{1,0:T(8,128)(2,1)} %bitcast.20, f32[4096,1]{1,0:T(8,128)} %copy.21.w, bf16[2048,512]{1,0:T(8,128)(2,1)} %bitcast.24, bf16[2048,512]{1,0:T(8,128)(2,1)} %bitcast.25, bf16[512,2048]{1,0:T(8,128)(2,1)} %bitcast.26), custom_call_target="tpu_custom_call" | custom-call | tf_op jit(solution)/shard_map/pallas_call | solution.py:267
  346.4 122.9 %shard_map.150 = f32[128,2048]{1,0:T(8,128)} custom-call(bf16[8,512,2048]{2,1,0:T(8,128)(2,1)} %bitcast.21), custom_call_target="tpu_custom_call" | custom-call | tf_op jit(solution)/shard_map/pallas_call | solution.py:353
  469.3 2.3 select_convert_fusion
  (25 shorter events, 2.1 us)
Async XLA Ops:
  6.5 1.6 copy-start
  6.5 16.2 %copy-start.4 = (f32[128,8]{0,1:T(8,128)S(1)}, f32[128,8]{0,1:T(8,128)}, u32[]{:S(2)}) copy-start(f32[128,8]{0,1:T(8,128)} %param.29) | copy-start | bytes 12292
  6.5 16.2 %copy-start.5 = (s32[128,8]{0,1:T(8,128)S(1)}, s32[128,8]{0,1:T(8,128)}, u32[]{:S(2)}) copy-start(s32[128,8]{0,1:T(8,128)} %param.28) | copy-start | bytes 12292
  6.5 216.3 %all-gather.2.cloned.1.call-start = ((), (), s32[]{:S(2)}) async-start(), calls=%async_computation | async-start | bytes 8650752 | tf_op jit(solution)/shard_map/all_gather | solution.py:416
  20.8 66.2 %copy-start.6 = (s32[8]{0:T(128)S(1)}, s32[8]{0:T(128)}, u32[]{:S(2)}) copy-start(s32[8]{0:T(128)} %lengths.1) | copy-start | bytes 100
  222.8 9.3 %copy-start.3 = (f32[2048]{0:T(1024)S(1)}, f32[2048]{0:T(1024)}, u32[]{:S(2)}) copy-start(f32[2048]{0:T(1024)} %param.24) | copy-start | bytes 24580
  232.1 2.0 copy-start.2
  346.4 125.3 %copy-start.1 = (bf16[512,2048]{1,0:T(8,128)(2,1)S(1)}, bf16[512,2048]{1,0:T(8,128)(2,1)}, u32[]{:S(2)}) copy-start(bf16[512,2048]{1,0:T(8,128)(2,1)} %param.20) | copy-start | bytes 6291460
Sparse Core Ops, SparseCore 0:
  10.2 80.3 all-gather.1

commit v2 on v1

--- a/solution.py
+++ b/solution.py
@@ -51,55 +51,77 @@
     return q, z, xn, yn, dg, other
 
 
-def first_kernel(nz, nq, tok, pre, tok_out, pre_out, zs, qs, ls):
+def choose_kernel(groups, src, dst):
+    dst[...] = src[...]
+
+
+def choose(group_of, cache):
+    block = (1,) + cache.shape[1:]
+    return pl.pallas_call(
+        choose_kernel,
+        out_shape=jax.ShapeDtypeStruct(group_of.shape + cache.shape[1:], cache.dtype),
+        grid_spec=pltpu.PrefetchScalarGridSpec(
+            num_scalar_prefetch=1,
+            grid=group_of.shape,
+            in_specs=[pl.BlockSpec(block, lambda r, g: (g[r], 0, 0))],
+            out_specs=pl.BlockSpec(block, lambda r, g: (r, 0, 0)),
+        ),
+    )(group_of, cache)
+
+
+def first_kernel(nz, nq, tok, pre, wts, tok_out, pre_out, wts_out, zs, qs, ws, vs, ls):
     q = lax.axis_index("req")
     z = lax.axis_index("exp")
     zp = [(q, lax.rem(z + j, nz)) for j in range(1, nz)]
     qp = [lax.rem(q + j, nq) for j in range(1, nq)]
     greet(zp + [(p, z) for p in qp])
-    copies = []
-    for i, peer in enumerate(zp):
-        c = remote(tok, tok_out.at[z], zs, i, peer)
-        c.start()
-        copies.append(c)
-    for i, p in enumerate(qp):
-        c = remote(pre.at[p], pre_out.at[q], qs, i, (p, z))
-        c.start()
-        copies.append(c)
-    for c in (
+    copies = [
+        pltpu.make_async_copy(wts, wts_out.at[q, z], ls.at[2]),
         pltpu.make_async_copy(tok, tok_out.at[z], ls.at[0]),
         pltpu.make_async_copy(pre.at[q], pre_out.at[q], ls.at[1]),
-    ):
+    ]
+    gathers = [remote(wts, wts_out.at[q, z], ws, i, peer) for i, peer in enumerate(zp)]
+    copies += [remote(tok, tok_out.at[z], zs, i, peer) for i, peer in enumerate(zp)]
+    copies += [remote(pre.at[p], pre_out.at[q], qs, i, (p, z)) for i, p in enumerate(qp)]
+    for c in gathers + copies:
         c.start()
-        copies.append(c)
-    for c in copies:
+    for c in gathers:
         c.wait()
-
-
-def first(tokens, outgoing, nz, nq):
+    copies[0].wait()
+    passed = [remote(wts_out.at[q], wts_out.at[q], vs, i, (p, z)) for i, p in enumerate(qp)]
+    for c in passed:
+        c.start()
+    for c in copies[1:] + passed:
+        c.wait()
+
+
+def first(tokens, outgoing, weights, nz, nq):
     return pl.pallas_call(
         functools.partial(first_kernel, nz, nq),
         out_shape=(
             jax.ShapeDtypeStruct((nz,) + tokens.shape, tokens.dtype),
             jax.ShapeDtypeStruct(outgoing.shape, outgoing.dtype),
+            jax.ShapeDtypeStruct((nq, nz) + weights.shape, weights.dtype),
         ),
-        in_specs=[ANY, ANY],
-        out_specs=(ANY, ANY),
+        in_specs=[ANY, ANY, ANY],
+        out_specs=(ANY, ANY, ANY),
         scratch_shapes=[
             pltpu.SemaphoreType.DMA((2, nz - 1)),
             pltpu.SemaphoreType.DMA((2, nq - 1)),
-            pltpu.SemaphoreType.DMA((2,)),
+            pltpu.SemaphoreType.DMA((2, nz - 1)),
+            pltpu.SemaphoreType.DMA((2, nq - 1)),
+            pltpu.SemaphoreType.DMA((3,)),
         ],
         compiler_params=pltpu.CompilerParams(collective_id=0, has_side_effects=True),
-    )(tokens, outgoing)
-
-
-def heads_kernel(nz, width, src, dst, zs, ls):
+    )(tokens, outgoing, weights)
+
+
+def heads_kernel(nz, src, dst, zs, ls):
     q = lax.axis_index("req")
     z = lax.axis_index("exp")
     peers = [(q, lax.rem(z + j, nz)) for j in range(1, nz)]
     greet(peers)
-    mine = dst.at[:, pl.ds(pl.multiple_of(z * width, width), width)]
+    mine = dst.at[z]
     copies = [remote(src, mine, zs, i, peer) for i, peer in enumerate(peers)]
     copies.append(pltpu.make_async_copy(src, mine, ls))
     for c in copies:
@@ -109,10 +131,9 @@
 
 
 def heads(attn, nz):
-    rows, width = attn.shape
-    return pl.pallas_call(
-        functools.partial(heads_kernel, nz, width),
-        out_shape=jax.ShapeDtypeStruct((rows, nz * width), attn.dtype),
+    return pl.pallas_call(
+        functools.partial(heads_kernel, nz),
+        out_shape=jax.ShapeDtypeStruct((nz,) + attn.shape, attn.dtype),
         in_specs=[ANY],
         out_specs=ANY,
         scratch_shapes=[pltpu.SemaphoreType.DMA((2, nz - 1)), pltpu.SemaphoreType.DMA],
@@ -277,24 +298,18 @@
     )(lengths, x, w, gate, up, down)
 
 
-def scatter_kernel(nz, parts, out, held, came, rx, ry, rz, sems, zs, ls):
+def scatter_kernel(nz, chunks, parts, out, held, came, rx, ry, rz, sems, zs, ls):
     q, z, xn, yn, dg, other = plane()
     slots, width = parts.shape[1:]
-    half = width // 2
+    chunk = width // chunks
+    half = chunk // 2
     mine_rows = slots // nz
-    left, right = pl.ds(0, half), pl.ds(half, half)
     tox, toy, sib = (xn, z), (yn, z), (q + other, z)
     peers = [lax.rem(z + j, nz) for j in range(1, nz)]
     greet([tox, toy, sib] + [(q, p) for p in peers])
     order = (dg, xn, yn, q)
     DG, XN, YN, ME = range(4)
-    swap = [remote(parts.at[r + other], came.at[k], sems, k, sib) for k, r in enumerate(order)]
-    load = [pltpu.make_async_copy(parts.at[r], held.at[k], ls.at[k]) for k, r in enumerate(order)]
-    for c in swap:
-        c.start()
-    for c in load:
-        c.start()
-    step = 64
+    step = 128
 
     def add(dst, src):
         @pl.loop(0, slots // step)
@@ -302,56 +317,101 @@
             at = pl.ds(pl.multiple_of(i * step, step), step)
             dst[at, :] = dst[at, :] + src[at, :]
 
-    x1 = remote(held.at[DG, :, left], rx.at[0], sems, 4, tox)
-    y1 = remote(held.at[DG, :, right], ry.at[0], sems, 5, toy)
-    x2 = remote(held.at[XN, :, left], rx.at[1], sems, 6, tox)
-    y2 = remote(held.at[YN, :, right], ry.at[1], sems, 7, toy)
-    x3 = remote(held.at[XN, :, right], rx.at[2], sems, 8, tox)
-    y3 = remote(held.at[YN, :, left], ry.at[2], sems, 9, toy)
-    for k, after in ((DG, (x1, y1)), (XN, (x2,)), (YN, (y2,)), (ME, ())):
-        swap[k].wait_recv()
-        load[k].wait()
-        add(held.at[k], came.at[k])
-        for c in after:
+    class Part:
+        pass
+
+    def describe(n):
+        p = Part()
+        p.cols = pl.ds(n * chunk, chunk)
+        left, right = pl.ds(n * chunk, half), pl.ds(n * chunk + half, half)
+        p.left, p.right = left, right
+        spot = pl.ds(n * half, half)
+        p.rx = [rx.at[i, :, spot] for i in range(3)]
+        p.ry = [ry.at[i, :, spot] for i in range(3)]
+        at = sems.at[n]
+        p.swap = [
+            remote(parts.at[r + other, :, p.cols], came.at[k, :, p.cols], at, k, sib)
+            for k, r in enumerate(order)
+        ]
+        p.load = [
+            pltpu.make_async_copy(parts.at[r, :, p.cols], held.at[k, :, p.cols], ls.at[n, k])
+            for k, r in enumerate(order)
+        ]
+        p.x1 = remote(held.at[DG, :, left], p.rx[0], at, 4, tox)
+        p.y1 = remote(held.at[DG, :, right], p.ry[0], at, 5, toy)
+        p.x2 = remote(held.at[XN, :, left], p.rx[1], at, 6, tox)
+        p.y2 = remote(held.at[YN, :, right], p.ry[1], at, 7, toy)
+        p.x3 = remote(held.at[XN, :, right], p.rx[2], at, 8, tox)
+        p.y3 = remote(held.at[YN, :, left], p.ry[2], at, 9, toy)
+        p.last = [
+            remote(
+                held.at[ME, pl.ds(pl.multiple_of(d * mine_rows, mine_rows), mine_rows), p.cols],
+                rz.at[i, :, p.cols],
+                zs.at[n],
+                i,
+                (q, d),
+            )
+            for i, d in enumerate(peers)
+        ]
+        return p
+
+    def cores(p):
+        for k, after in ((DG, (p.x1, p.y1)), (XN, (p.x2,)), (YN, (p.y2,)), (ME, ())):
+            p.swap[k].wait_recv()
+            p.load[k].wait()
+            add(held.at[k, :, p.cols], came.at[k, :, p.cols])
+            for c in after:
+                c.start()
+
+    def turn(p):
+        p.x1.wait_recv()
+        add(held.at[YN, :, p.left], p.rx[0])
+        p.y3.start()
+        p.y1.wait_recv()
+        add(held.at[XN, :, p.right], p.ry[0])
+        p.x3.start()
+
+    def finish(p):
+        p.x2.wait_recv()
+        add(held.at[ME, :, p.left], p.rx[1])
+        p.y2.wait_recv()
+        add(held.at[ME, :, p.right], p.ry[1])
+        p.y3.wait_recv()
+        add(held.at[ME, :, p.left], p.ry[2])
+        p.x3.wait_recv()
+        add(held.at[ME, :, p.right], p.rx[2])
+        for c in p.last:
             c.start()
-    x1.wait_recv()
-    add(held.at[YN, :, left], rx.at[0])
-    y3.start()
-    y1.wait_recv()
-    add(held.at[XN, :, right], ry.at[0])
-    x3.start()
-    x2.wait_recv()
-    add(held.at[ME, :, left], rx.at[1])
-    y2.wait_recv()
-    add(held.at[ME, :, right], ry.at[1])
-
-    def shard(p, cols):
-        return held.at[ME, pl.ds(pl.multiple_of(p * mine_rows, mine_rows), mine_rows), cols]
-
-    sent = []
-    for side, cols, c, came_in in ((0, left, y3, ry.at[2]), (1, right, x3, rx.at[2])):
-        c.wait_recv()
-        add(held.at[ME, :, cols], came_in)
-        for i, p in enumerate(peers):
-            s = remote(shard(p, cols), rz.at[i, :, cols], zs, side * (nz - 1) + i, (q, p))
-            s.start()
-            sent.append(s)
-    own = shard(z, slice(None))
-    for s in sent:
-        s.wait()
-    total = own[...].astype(jnp.float32)
-    for i in range(nz - 1):
-        total += rz[i].astype(jnp.float32)
-    out[...] = total
-    for c in swap + [x1, y1, x2, y2, x3, y3]:
-        c.wait_send()
+
+    pieces = [describe(n) for n in range(chunks)]
+    for p in pieces:
+        for c in p.swap + p.load:
+            c.start()
+    for n in range(chunks + 2):
+        if n < chunks:
+            cores(pieces[n])
+        if 1 <= n <= chunks:
+            turn(pieces[n - 1])
+        if n >= 2:
+            finish(pieces[n - 2])
+    own = pl.ds(pl.multiple_of(z * mine_rows, mine_rows), mine_rows)
+    for p in pieces:
+        for c in p.last:
+            c.wait()
+        total = held[ME, own, p.cols].astype(jnp.float32)
+        for i in range(nz - 1):
+            total += rz[i, :, p.cols].astype(jnp.float32)
+        out[:, p.cols] = total
+        for c in p.swap + [p.x1, p.y1, p.x2, p.y2, p.x3, p.y3]:
+            c.wait_send()
 
 
 def scatter(parts, nz):
     nq, slots, width = parts.shape
     bf = jnp.bfloat16
-    return pl.pallas_call(
-        functools.partial(scatter_kernel, nz),
+    chunks = 4
+    return pl.pallas_call(
+        functools.partial(scatter_kernel, nz, chunks),
         out_shape=jax.ShapeDtypeStruct((slots // nz, width), jnp.float32),
         in_specs=[ANY],
         out_specs=pl.BlockSpec(memory_space=pltpu.VMEM),
@@ -361,9 +421,9 @@
             pltpu.VMEM((3, slots, width // 2), bf),
             pltpu.VMEM((3, slots, width // 2), bf),
             pltpu.VMEM((nz - 1, slots // nz, width), bf),
-            pltpu.SemaphoreType.DMA((2, 10)),
-            pltpu.SemaphoreType.DMA((2, 2 * (nz - 1))),
-            pltpu.SemaphoreType.DMA((4,)),
+            pltpu.SemaphoreType.DMA((chunks, 2, 10)),
+            pltpu.SemaphoreType.DMA((chunks, 2, nz - 1)),
+            pltpu.SemaphoreType.DMA((chunks, 4)),
         ],
         compiler_params=pltpu.CompilerParams(
             collective_id=3, has_side_effects=True, vmem_limit_bytes=56 * 2**20
@@ -400,13 +460,14 @@
 
     groups, piece, _, _ = prefix_cache.shape
     flat_cache = prefix_cache.reshape(groups, piece, 2 * local)
-    outgoing = jnp.stack(
-        [lax.dynamic_index_in_dim(flat_cache, group_of[r], 0, keepdims=False) for r in range(nq)]
-    )
+    outgoing = choose(group_of, flat_cache)
+    named = jnp.arange(experts, dtype=jnp.int32)[:, None, None] == routes.T[None]
+    dense = jnp.sum(jnp.where(named, route_weights.T[None], 0.0), axis=1)
     if paths:
-        mine, arrived = first(tokens, outgoing, nz, nq)
+        mine, arrived, every_weight = first(tokens, outgoing, dense, nz, nq)
     else:
         mine = lax.all_gather(tokens, "exp", axis=0)
+        every_weight = lax.all_gather(dense, BOTH, axis=0).reshape(nq, nz, experts, rows_dev)
         arrived = lax.all_to_all(outgoing, "req", split_axis=0, concat_axis=0, tiled=True)
     mine = mine.reshape(slots, width)
     arrived = arrived.reshape(nq * piece, 2 * local)
@@ -415,13 +476,9 @@
     w_part = lax.dynamic_slice_in_dim(w_out, q * share, share, 0)
     w_whole = lax.all_gather(w_part, ("exp", "req"), axis=0, tiled=True)
 
-    named = routes[:, :, None] == jnp.arange(experts, dtype=jnp.int32)
-    dense = jnp.sum(jnp.where(named, route_weights[:, :, None], 0.0), axis=1)
-    dense = lax.all_gather(dense, BOTH, axis=0, tiled=True)
     expert = (q * nz + z) // 2
-    weight = jnp.sum(
-        jnp.where(jnp.arange(experts, dtype=jnp.int32) == expert, dense, 0.0), axis=1, keepdims=True
-    )
+    every_weight = lax.dynamic_index_in_dim(every_weight, expert, 2, keepdims=False)
+    weight = every_weight.reshape(nq * slots, 1)
 
     half = HD // 2
     freqs = 10000.0 ** (-(jnp.arange(half, dtype=jnp.float32) * 2.0) / HD)
@@ -436,7 +493,8 @@
     attn = attend(
         length, mine, attn_gain[None, :], w_query, w_key, w_value, cosine, sine, arrived
     )
-    attn = heads(attn, nz) if paths else lax.all_gather(attn, "exp", axis=1, tiled=True)
+    attn = heads(attn, nz) if paths else lax.all_gather(attn, "exp", axis=0)
+    attn = jnp.moveaxis(attn, 0, 1).reshape(slots, nz * local)
     attn_out = jnp.dot(attn, w_whole, preferred_element_type=jnp.float32)
     hidden = (mine.astype(jnp.float32) + attn_out).astype(jnp.bfloat16)
     normed2 = norm_rows(hidden, moe_gain).astype(jnp.bfloat16)

time: 479 us -> 395 us (0.82)
  blocking collectives: 62.2 us -> 0 us
  between operations: 29 us -> 13.5 us
  Pallas kernels: 357 us -> 349 us
    all_gather x1 -> x0, blocking collectives: 62.2 us -> none  [on_device(): dense = lax.all_gather(dense, BOTH, axis=0, tiled=True)]
    pallas_call x2 -> x3, Pallas kernels: 170 us -> 154 us  [the longest x1 92.1 us: scatter(): pl.pallas_call(functools.partial(scatter_kernel, nz, chunks), out_shape=j...]
    pallas_call x1, Pallas kernels: 54.3 us -> 65 us  [first(): pl.pallas_call(functools.partial(first_kernel, nz, nq), out_shape=(jax.Sh...]
    unnamed x21 -> x14, local copies, waits for them, and re-layouts: 6.7 us -> 1.61 us
  transfers between devices with their start and end apart: 1 -> 1, of which waited for: 0 -> 0; matrix products, arithmetic and copies ran while one was open for 3% -> 3% of each run, Pallas kernels for 25% -> 38%
where the time goes in v2:
time: 395 us; the launch traced here: 392 us
  Pallas kernels  349 us (88%)
  between operations  13.5 us (3%)
  local copies, waits for them, and re-layouts  12.7 us (3%)
  matrix products  9.57 us (2%)
  other arithmetic  7.55 us (2%)
    pallas_call x1, Pallas kernels, scatter(): pl.pallas_call(functools.partial(scatter_kernel, nz, chunks), out_shape=j...  92.1 us
    pallas_call x1, Pallas kernels, gather(): pl.pallas_call(gather_kernel, out_shape=jax.ShapeDtypeStruct((nq,) + rows...  75.6 us
    pallas_call x1, Pallas kernels, first(): pl.pallas_call(functools.partial(first_kernel, nz, nq), out_shape=(jax.Sh...  65 us
    pallas_call x1, Pallas kernels, heads(): pl.pallas_call(functools.partial(heads_kernel, nz), out_shape=jax.ShapeDt...  56.2 us
    pallas_call x1, Pallas kernels, experts_on(): pl.pallas_call(expert_kernel, out_shape=jax.ShapeDtypeStruct((count, widt...  34.1 us
    pallas_call x1, Pallas kernels, attend(): pl.pallas_call(attend_kernel, out_shape=jax.ShapeDtypeStruct((rows, local...  20 us
    dot_general x1, matrix products, on_device(): attn_out = jnp.dot(attn, w_whole, preferred_element_type=jnp.float32)  9.57 us
  transfers between devices with their start and end apart: 1, of which 0 were waited for; matrix products, arithmetic and copies ran while one was open for 3% of the time, Pallas kernels for 38%

profile of v2, /device:TPU:9, one launch (start us, length us, event | category | flops | bytes accessed | tf_op | source)
XLA Modules:
  0.0 392.3 jit_solution(8964774525905006843)
XLA Ops:
  6.5 1.6 copy-done
  8.1 0.7 constant_dynamic-slice_fusion.1
  8.9 0.0 all-gather.2.cloned.1.call-update
  8.9 2.6 reshape.50.src
  11.5 0.6 dynamic_slice.13.length
  12.2 6.0 %shard_map.145.pre = bf16[8,128,1024]{2,1,0:T(8,128)(2,1)} custom-call(s32[8]{0:T(128)} %groups.1, bf16[4,128,1024]{2,1,0:T(8,128)(2,1)} %reshape.50.src), custom_call_target="tpu_custom_call" | custom-call | tf_op jit(solution)/shard_map/pallas_call | solution.py:60
  18.2 0.6 select_reduce_fusion.wts
  18.8 65.0 %shard_map.146 = (bf16[4,128,2048]{2,1,0:T(8,128)(2,1)}, bf16[8,128,1024]{2,1,0:T(8,128)(2,1)}, f32[8,4,16,128]{3,2,1,0:T(8,128)}) custom-call(bf16[128,2048]{1,0:T(8,128)(2,1)} %tok.1, bf16[8,128,1024]{2,1,0:T(8,128)(2,1)} %shard_map.145.pre, f32[16,128]{1,0:T(8,128)} %select_reduce_fusion.wts), custom_call_target="tpu_custom_call" | custom-call | tf_op jit(solution)/shard_map/pallas_call | solution.py:99
  83.8 1.0 fusion.3
  84.8 1.0 pad_maximum_fusion
  85.8 20.0 %shard_map.147.src = bf16[512,512]{1,0:T(8,128)(2,1)} custom-call(s32[1]{0:T(128)} %dynamic_slice.13.length, bf16[512,2048]{1,0:T(8,128)(2,1)} %bitcast.25, f32[1,2048]{1,0:T(1,128)} %bitcast.28, bf16[2048,512]{1,0:T(8,128)(2,1)} %wq.1, bf16[2048,512]{1,0:T(8,128)(2,1)} %wk.1, bf16[2048,512]{1,0:T(8,128)(2,1)} %wv.1, f32[512,128]{1,0:T(8,128)} %get-tuple-element.16.cosine, ...), custom_call_target="tpu_custom_call" | custom-call | tf_op jit(solution)/shard_map/pallas_call | solution.py:186
  105.9 56.2 %shard_map.148 = bf16[4,512,512]{2,1,0:T(8,128)(2,1)} custom-call(bf16[512,512]{1,0:T(8,128)(2,1)} %shard_map.147.src), custom_call_target="tpu_custom_call" | custom-call | tf_op jit(solution)/shard_map/pallas_call | solution.py:134
  162.0 4.2 %copy.18 = bf16[512,4,512]{0,2,1:T(8,128)(2,1)} copy(bf16[512,4,512]{2,0,1:T(8,128)(2,1)} %bitcast.18) | data formatting | bytes 4194304 | tf_op jit(solution)/shard_map/transpose | solution.py:497
  166.2 0.9 constant_dynamic-slice_fusion
  167.1 2.0 copy.19.w
  169.1 0.6 add_compare_fusion
  169.8 0.0 all-gather.2.cloned.1.call-done
  169.8 0.0 copy-start.3
  169.8 9.6 %fusion = (f32[512]{0:T(512)S(1)}, bf16[512,2048]{1,0:T(8,128)(2,1)S(1)}) fusion(bf16[512,2048]{0,1:T(8,128)(2,1)} %bitcast.24, bf16[2048,2048]{1,0:T(8,128)(2,1)} %all-gather.2.cloned.1.call-done, bf16[512,2048]{1,0:T(8,128)(2,1)} %bitcast.26), kind=kOutput, calls=%fused_computation.2 | convolution fusion | flops 4301258240 | bytes 14682112 | tf_op jit(solution)/shard_map/dot_general | solution.py:498
  179.4 1.9 fusion.2.src
  181.4 75.6 %shard_map.149 = bf16[8,512,2048]{2,1,0:T(8,128)(2,1)} custom-call(bf16[512,2048]{1,0:T(8,128)(2,1)} %fusion.2.src), custom_call_target="tpu_custom_call" | custom-call | tf_op jit(solution)/shard_map/pallas_call | solution.py:254
  256.9 34.1 %shard_map.150 = bf16[4096,2048]{1,0:T(8,128)(2,1)} custom-call(s32[8]{0:T(128)} %lengths.1, bf16[4096,2048]{1,0:T(8,128)(2,1)} %bitcast.16, f32[4096,1]{1,0:T(8,128)} %copy.19.w, bf16[2048,512]{1,0:T(8,128)(2,1)} %bitcast.21, bf16[2048,512]{1,0:T(8,128)(2,1)} %bitcast.22, bf16[512,2048]{1,0:T(8,128)(2,1)} %bitcast.23), custom_call_target="tpu_custom_call" | custom-call | tf_op jit(solution)/shard_map/pallas_call | solution.py:288
  291.1 92.1 %shard_map.151 = f32[128,2048]{1,0:T(8,128)} custom-call(bf16[8,512,2048]{2,1,0:T(8,128)(2,1)} %bitcast.17), custom_call_target="tpu_custom_call" | custom-call | tf_op jit(solution)/shard_map/pallas_call | solution.py:413
  383.2 2.3 select_convert_fusion
  (16 shorter events, 0.0 us)
Async XLA Ops:
  6.5 1.6 copy-start
  6.5 5.0 %copy-start.6 = (s32[8]{0:T(128)S(1)}, s32[8]{0:T(128)}, u32[]{:S(2)}) copy-start(s32[8]{0:T(128)} %lengths.1) | copy-start | bytes 100
  6.5 163.2 %all-gather.2.cloned.1.call-start = ((), (), s32[]{:S(2)}) async-start(), calls=%async_computation | async-start | bytes 8650752 | tf_op jit(solution)/shard_map/all_gather | solution.py:477
  11.5 6.7 %copy-start.4 = (f32[128,8]{0,1:T(8,128)S(1)}, f32[128,8]{0,1:T(8,128)}, u32[]{:S(2)}) copy-start(f32[128,8]{0,1:T(8,128)} %param.29) | copy-start | bytes 12292
  11.5 6.7 %copy-start.5 = (s32[128,8]{0,1:T(8,128)S(1)}, s32[128,8]{0,1:T(8,128)}, u32[]{:S(2)}) copy-start(s32[128,8]{0,1:T(8,128)} %param.28) | copy-start | bytes 12292
  169.8 9.6 %copy-start.3 = (f32[2048]{0:T(1024)S(1)}, f32[2048]{0:T(1024)}, u32[]{:S(2)}) copy-start(f32[2048]{0:T(1024)} %param.24) | copy-start | bytes 24580
  179.4 2.0 copy-start.2
  291.1 94.4 %copy-start.1 = (bf16[512,2048]{1,0:T(8,128)(2,1)S(1)}, bf16[512,2048]{1,0:T(8,128)(2,1)}, u32[]{:S(2)}) copy-start(bf16[512,2048]{1,0:T(8,128)(2,1)} %param.20) | copy-start | bytes 6291460
Sparse Core Ops, SparseCore 0:
  10.2 121.6 all-gather.1
